TPU v7x, 512 devices: a whole 4x4x16 slice. The times are simulated.
512 devices in a mesh: rows: 32 (over z, core), feat: 16 (over y, x).
Axes of the slice: x: 4, y: 4, z: 16, core: 2. Of those that a mesh axis runs over, the one named last changes fastest.
Arguments:
- features: bfloat16 [163840, 8192], P('rows', 'feat'), may hold values from -0.015625 to 0.015625
- targets: float32 [163840], P('rows'), may hold values from -6 to 6
- target_noise: float32 [96, 163840], P(None, 'rows'), may hold values from -6 to 6
- prior_noise: float32 [96, 8192], P(None, 'feat'), may hold values from -6 to 6
- precision: float32 [8192], P('feat'), may hold values from 0.5 to 2
Outputs:
- sampled_coefficients: float32 [96, 8192], P(None, 'feat')
- residual: float32 [96, 8192], P(None, 'feat')
All inputs are finite; a program needn't handle non-finite values.
Results may differ from a plain program's by a relative error of at most 0.025.
Values may be sent and summed in bfloat16 or wider, within the bound.
No kernel may reach another device: no remote copies, remote signals or barrier semaphores. Data moves between devices by JAX's collectives and lax.ppermute only.
A program may use at most 64 MiB of HBM per device.

v0:
```python
import jax
import jax.numpy as jnp
from jax import lax
from jax.sharding import PartitionSpec as P

ITERS = 2


def norms(residual):
    return lax.psum(jnp.sum(residual * residual, axis=1), "feat")


def split_terms(error_terms):
    high = error_terms.astype(jnp.bfloat16)
    low = (error_terms - high.astype(jnp.float32)).astype(jnp.bfloat16)
    return jnp.concatenate([high, low], axis=0)


def shards(features, targets, target_noise, prior_noise, precision):
    draws = prior_noise.shape[0]
    perturbed_targets = targets[None, :] + target_noise

    def image(direction):
        partial_rows = jnp.einsum(
            "sd,rd->sr",
            direction.astype(jnp.bfloat16),
            features,
            preferred_element_type=jnp.float32,
        )
        return lax.psum(partial_rows, "feat")

    def back(error_terms):
        stacked = jnp.einsum(
            "sr,rd->sd", split_terms(error_terms), features, preferred_element_type=jnp.float32
        )
        partial_cols = stacked[:draws] + stacked[draws:]
        return lax.psum(partial_cols, "rows")

    prior_sample = prior_noise * lax.rsqrt(precision)[None, :]
    fitted = image(prior_sample)
    error_terms = perturbed_targets - fitted
    residual = back(error_terms)
    direction = residual
    solution = prior_sample
    norm_now = norms(residual)
    for step in range(ITERS):
        operator_result = back(image(direction)) + precision[None, :] * direction
        curve = lax.psum(jnp.sum(direction * operator_result, axis=1), "feat")
        alpha = norm_now / curve
        solution = solution + alpha[:, None] * direction
        residual = residual - alpha[:, None] * operator_result
        norm_next = norms(residual)
        direction = residual + (norm_next / norm_now)[:, None] * direction
        norm_now = norm_next
    return (solution, residual)


def solution(mesh):
    return jax.shard_map(
        shards,
        mesh=mesh,
        in_specs=(P("rows", "feat"), P("rows"), P(None, "rows"), P(None, "feat"), P("feat")),
        out_specs=(P(None, "feat"), P(None, "feat")),
        check_vma=False,
    )
```

profile of v0, /device:TPU:1, one launch (start us, length us, event | category | flops | bytes accessed | tf_op | source)
XLA Modules:
  0.0 1118.5 jit_solution(7999580476240981985)
XLA Ops:
  7.9 5.6 fusion.13
  13.6 124.2 %all-reduce.8.cloned.1.call-done = f32[96,5120]{1,0:T(8,128)} async-done(((f32[96,5120]{1,0:T(8,128)}), f32[96,5120]{1,0:T(8,128)}) %all-reduce.8.cloned.1.call-update) | async-done | bytes 1966096 | tf_op jit(solution)/shard_map/psum | solution.py:30
  137.8 2.1 fusion.12
  139.8 1.0 copy-done
  140.9 1.2 fusion
  142.0 0.7 slice_add_fusion.2
  142.8 199.2 %all-reduce.10.cloned.1.call-done = f32[96,512]{1,0:T(8,128)} async-done(((f32[96,512]{1,0:T(8,128)}), f32[96,512]{1,0:T(8,128)}) %all-reduce.10.cloned.1.call-update) | async-done | bytes 196624 | tf_op jit(solution)/shard_map/psum | solution.py:37
  342.0 5.6 fusion.16
  347.6 117.8 %all-reduce.12.cloned.1.call-done = f32[96,5120]{1,0:T(8,128)} async-done(((f32[96,5120]{1,0:T(8,128)}), f32[96,5120]{1,0:T(8,128)}) %all-reduce.12.cloned.1.call-update) | async-done | bytes 1966096 | tf_op jit(solution)/shard_map/psum | solution.py:30
  465.4 2.4 subtract_convert_fusion.1
  467.8 3.7 fusion.4
  472.3 199.2 %all-reduce.14.cloned.1.call-done = f32[96,512]{1,0:T(8,128)} async-done(((f32[96,512]{1,0:T(8,128)}), f32[96,512]{1,0:T(8,128)}) %all-reduce.14.cloned.1.call-update) | async-done | bytes 196624 | tf_op jit(solution)/shard_map/psum | solution.py:37
  671.5 1.1 multiply_reduce_fusion.2
  672.6 33.1 %all-reduce = (f32[96]{0:T(128)S(1)}, f32[96]{0:T(128)S(1)}) all-reduce(f32[96]{0:T(128)S(1)} %get-tuple-element.3, f32[96]{0:T(128)S(1)} %get-tuple-element.2), channel_id=1, replica_groups=mesh['rows'=32,'feat'=16] {'feat'}, use_global_device_ids=true, to_apply=%region_3.0 | all-reduce | flops 192 | bytes 1536 | tf_op jit(solution)/shard_map/psum | solution.py:10
  705.6 1.1 multiply_reduce_fusion.1
  706.8 28.5 %psum.76 = f32[96]{0:T(128)S(1)} all-reduce(f32[96]{0:T(128)S(1)} %multiply_reduce_fusion.1), channel_id=1, replica_groups=mesh['rows'=32,'feat'=16] {'feat'}, use_global_device_ids=true, to_apply=%region_9.0 | all-reduce | flops 96 | bytes 768 | tf_op jit(solution)/shard_map/psum | solution.py:10
  735.3 5.6 fusion.14
  741.0 128.5 %all-reduce.16.cloned.1.call-done = f32[96,5120]{1,0:T(8,128)} async-done(((f32[96,5120]{1,0:T(8,128)}), f32[96,5120]{1,0:T(8,128)}) %all-reduce.16.cloned.1.call-update) | async-done | bytes 1966096 | tf_op jit(solution)/shard_map/psum | solution.py:30
  869.5 2.4 subtract_convert_fusion
  871.9 3.7 fusion.8
  876.4 199.2 %all-reduce.18.cloned.1.call-done = f32[96,512]{1,0:T(8,128)} async-done(((f32[96,512]{1,0:T(8,128)}), f32[96,512]{1,0:T(8,128)}) %all-reduce.18.cloned.1.call-update) | async-done | bytes 196624 | tf_op jit(solution)/shard_map/psum | solution.py:37
  1075.6 1.2 multiply_reduce_fusion
  1076.7 33.1 %psum.79 = f32[96]{0:T(128)S(1)} all-reduce(f32[96]{0:T(128)S(1)} %multiply_reduce_fusion), channel_id=1, replica_groups=mesh['rows'=32,'feat'=16] {'feat'}, use_global_device_ids=true, to_apply=%region_13.0 | all-reduce | flops 96 | bytes 768 | tf_op jit(solution)/shard_map/psum | solution.py:48
  1109.8 1.8 multiply_subtract_fusion
  (31 shorter events, 2.5 us)
Async XLA Ops:
  7.2 130.6 %all-reduce.8.cloned.1.call-start = ((), (), s32[]{:S(2)}) async-start(), calls=%async_computation | async-start | bytes 3932160 | tf_op jit(solution)/shard_map/psum | solution.py:30
  7.9 129.9 %copy-start.6 = (f32[5120]{0:T(1024)S(1)}, f32[5120]{0:T(1024)}, u32[]{:S(2)}) copy-start(f32[5120]{0:T(1024)} %param.6) | copy-start | bytes 61444
  13.5 124.3 %copy-start.3 = (f32[96,5120]{1,0:T(8,128)S(1)}, f32[96,5120]{1,0:T(8,128)}, u32[]{:S(2)}) copy-start(f32[96,5120]{1,0:T(8,128)} %param.7) | copy-start | bytes 5898244
  13.5 328.5 %all-reduce.10.cloned.1.call-start = ((), (), s32[]{:S(2)}) async-start(), calls=%async_computation.1 | async-start | bytes 393216 | tf_op jit(solution)/shard_map/psum | solution.py:37
  137.8 3.1 copy-start
  142.8 322.6 %all-reduce.12.cloned.1.call-start = ((), (), s32[]{:S(2)}) async-start(), calls=%async_computation.2 | async-start | bytes 3932160 | tf_op jit(solution)/shard_map/psum | solution.py:30
  347.6 323.9 %all-reduce.14.cloned.1.call-start = ((), (), s32[]{:S(2)}) async-start(), calls=%async_computation.3 | async-start | bytes 393216 | tf_op jit(solution)/shard_map/psum | solution.py:37
  467.8 203.7 %copy-start.1 = (f32[96,512]{1,0:T(8,128)S(1)}, f32[96,512]{1,0:T(8,128)}, u32[]{:S(2)}) copy-start(f32[96,512]{1,0:T(8,128)} %all-reduce.10.cloned.1.call-done) | copy-start | bytes 589828
  467.8 203.7 %copy-start.5 = (f32[512]{0:T(512)S(1)}, f32[512]{0:T(512)}, u32[]{:S(2)}) copy-start(f32[512]{0:T(512)} %param.9) | copy-start | bytes 6148
  472.3 397.2 %all-reduce.16.cloned.1.call-start = ((), (), s32[]{:S(2)}) async-start(), calls=%async_computation.4 | async-start | bytes 3932160 | tf_op jit(solution)/shard_map/psum | solution.py:30
  740.9 334.7 %all-reduce.18.cloned.1.call-start = ((), (), s32[]{:S(2)}) async-start(), calls=%async_computation.5 | async-start | bytes 393216 | tf_op jit(solution)/shard_map/psum | solution.py:37
  871.9 203.7 %copy-start.2 = (f32[96,512]{1,0:T(8,128)S(1)}, f32[96,512]{1,0:T(8,128)}, u32[]{:S(2)}) copy-start(f32[96,512]{1,0:T(8,128)} %all-reduce.14.cloned.1.call-done) | copy-start | bytes 589828
  871.9 238.0 %copy-start.4 = (f32[96,512]{1,0:T(8,128)S(1)}, f32[96,512]{1,0:T(8,128)}, u32[]{:S(2)}) copy-start(f32[96,512]{1,0:T(8,128)} %param.8) | copy-start | bytes 589828
Sparse Core Ops, SparseCore 0:
  13.6 124.0 all-reduce.7
  142.9 199.0 all-reduce.9
  347.7 117.6 all-reduce.11
  472.4 199.0 all-reduce.13
  741.1 128.3 all-reduce.15
  876.5 199.0 all-reduce.17
where the time goes:
time: 1120 us
  waiting for transfers between devices  968 us (86%)
  blocking collectives  94.7 us (8%)
  matrix products  25.4 us (2%)
  other arithmetic  14.2 us (1%)
  between operations  14.2 us (1%)
    psum x3, waiting for transfers between devices, back(): return lax.psum(partial_cols, 'rows')  598 us
    psum x3, waiting for transfers between devices, image(): return lax.psum(partial_rows, 'feat')  370 us
    psum x2, blocking collectives, norms(): return lax.psum(jnp.sum(residual * residual, axis=1), 'feat')  61.6 us
    psum x1, blocking collectives, shards(): curve = lax.psum(jnp.sum(direction * operator_result, axis=1), 'feat')  33.1 us
  transfers between devices with their start and end apart: 6, of which 6 were waited for; matrix products, arithmetic and copies ran while one was open for 0% of the time, Pallas kernels for 0%

commit v1 on v0

v1 whole, which is shorter than its diff:
```python
import functools
import math

import jax
import jax.numpy as jnp
from jax import lax
from jax.experimental import pallas as pl
from jax.experimental.pallas import tpu as pltpu
from jax.sharding import PartitionSpec as P

CORES = 2
LANES = 128
BLOCKS = 4
F32, BF16 = jnp.float32, jnp.bfloat16
MOST = 16 * 2**20
WHOLE = 56 * 2**20
SCALARS = 16
LITTLE = 8 * 2**20
IN_VMEM = pl.BlockSpec(memory_space=pltpu.VMEM)
SMALL = pl.CostEstimate(flops=2**16, bytes_accessed=2**22, transcendentals=0)


def lane_index(rows):
    return lax.broadcasted_iota(jnp.int32, (rows, LANES), 1)


def column_to_row(column):
    rows = column.shape[0]
    at = lax.broadcasted_iota(jnp.int32, (rows, LANES), 0) == lane_index(rows)
    return jnp.sum(jnp.where(at, column, 0.0), axis=0, keepdims=True)


def row_to_column(row, rows, first=0):
    at = lax.broadcasted_iota(jnp.int32, (rows, LANES), 0) + first == lane_index(rows)
    return jnp.sum(jnp.where(at, row, 0.0), axis=1, keepdims=True)


def split(value):
    high = value.astype(BF16).astype(F32)
    return high, value - high


def assemble(pieces_ref, whole):
    tall = pieces_ref.shape[1]
    across = whole.shape[1] // LANES
    for m in range(pieces_ref.shape[0]):
        i, j = divmod(m, across)
        whole[pl.ds(i * tall, tall), pl.ds(j * LANES, LANES)] = pieces_ref[m].astype(F32)


def multiply_out(value, f_ref, store, wide, copies=None):
    chunks = f_ref.shape[0] // wide
    blocks = math.gcd(chunks, BLOCKS)
    per = chunks // blocks
    size = per * wide
    for k in range(blocks):
        if copies is not None:
            copies[k].wait()
        terms = lax.dot_general(
            value,
            f_ref[pl.ds(k * size, size)],
            (((1,), (1,)), ((), ())),
            preferred_element_type=F32,
        )
        for c in range(per):
            store(k * per + c, terms[:, c * wide : (c + 1) * wide])


def fetch(f_hbm, kept_ref, sems):
    count = sems.shape[0]
    size = f_hbm.shape[0] // count
    copies = []
    for k in range(count):
        at = pl.ds(k * size, size)
        copies.append(pltpu.make_async_copy(f_hbm.at[at], kept_ref.at[at], sems.at[k]))
        copies[k].start()
    return copies


def multiply_into(value, f_ref, pieces_ref, first, copies=None):
    def store(c, part):
        pieces_ref[first + c] = part.astype(BF16)

    multiply_out(value, f_ref, store, pieces_ref.shape[2], copies)


def own_image_kernel(
    core_ref, noise_ref, scale_ref, own_hbm, pieces_ref, value_ref, kept_ref, sems
):
    copies = fetch(own_hbm, kept_ref, sems)
    draws = pieces_ref.shape[1]
    first = pl.multiple_of(core_ref[0] * draws, 8)
    value = (noise_ref[pl.ds(first, draws)] * lax.rsqrt(scale_ref[...])).astype(BF16)
    value_ref[...] = value
    multiply_into(value, kept_ref, pieces_ref, 0, copies)


def other_image_kernel(value_ref, half_ref, other_hbm, pieces_ref, kept_ref, sems):
    copies = fetch(other_hbm, kept_ref, sems)
    count = half_ref.shape[0]
    for c in range(count):
        pieces_ref[c] = half_ref[c]
    multiply_into(value_ref[...], kept_ref, pieces_ref, count, copies)


def image_kernel(count, scale_ref, own_ref, other_ref, *refs):
    vectors, (pieces_ref, sums_ref), wholes = (
        refs[:count],
        refs[count : count + 2],
        refs[count + 2 :],
    )
    for source, whole in zip(vectors, wholes):
        assemble(source, whole)
    value = wholes[0][...]
    direction = value.astype(BF16)
    multiply_into(direction, own_ref, pieces_ref, 0)
    multiply_into(direction, other_ref, pieces_ref, pieces_ref.shape[0] // CORES)
    sums = [value * value, value * value * scale_ref[...]]
    if count > 1:
        sums.append(value * wholes[1][...])
    lines = []
    for product in sums:
        column = jnp.sum(product, axis=1, keepdims=True)
        lines += [column_to_row(part) for part in split(column)]
    lines.append(jnp.zeros((SCALARS - len(lines), LANES), F32))
    sums_ref[...] = jnp.concatenate(lines, axis=0).astype(BF16)


def matmul_cost(draws, rows, width):
    return pl.CostEstimate(
        flops=2 * draws * rows * width, bytes_accessed=2 * rows * width, transcendentals=0
    )


def first_image_terms(core, noise, scale, own, other, n_feat):
    rows, width = own.shape
    draws = noise.shape[0] // CORES
    shape = (n_feat // CORES, draws, CORES * rows // n_feat)
    anywhere = [pl.BlockSpec(memory_space=pl.ANY)]
    kept = jax.ShapeDtypeStruct((rows, width), BF16)
    sems = [pltpu.SemaphoreType.DMA((math.gcd(shape[0], BLOCKS),))]
    params = pltpu.CompilerParams(vmem_limit_bytes=WHOLE)
    half, value = pl.pallas_call(
        own_image_kernel,
        in_specs=[pl.BlockSpec(memory_space=pltpu.SMEM)] + [IN_VMEM] * 2 + anywhere,
        out_specs=[IN_VMEM] * 2,
        out_shape=[
            jax.ShapeDtypeStruct(shape, BF16),
            jax.ShapeDtypeStruct((draws, width), BF16),
        ],
        scratch_shapes=[pltpu.VMEM((rows, width), BF16)] + sems,
        compiler_params=params,
        cost_estimate=matmul_cost(draws, rows, width),
    )(core, noise, scale, own)
    params = pltpu.CompilerParams(vmem_limit_bytes=MOST)
    terms, other = pl.pallas_call(
        other_image_kernel,
        in_specs=[IN_VMEM] * 2 + anywhere,
        out_specs=[IN_VMEM] * 2,
        out_shape=[jax.ShapeDtypeStruct((n_feat,) + shape[1:], BF16), kept],
        scratch_shapes=sems,
        compiler_params=params,
        cost_estimate=matmul_cost(draws, rows, width),
    )(value, half, other)
    return terms, other


def image_terms(scale, own, other, vectors, n_feat):
    rows, width = own.shape
    draws = vectors[0].size // width
    count = len(vectors)
    return pl.pallas_call(
        functools.partial(image_kernel, count),
        in_specs=[IN_VMEM] * (3 + count),
        out_specs=[IN_VMEM] * 2,
        out_shape=[
            jax.ShapeDtypeStruct((n_feat, draws, CORES * rows // n_feat), BF16),
            jax.ShapeDtypeStruct((SCALARS, LANES), BF16),
        ],
        scratch_shapes=[pltpu.VMEM((draws, width), F32)] * count,
        compiler_params=pltpu.CompilerParams(vmem_limit_bytes=MOST),
        cost_estimate=matmul_cost(draws, CORES * rows, width),
    )(scale, own, other, *vectors)


def sum_kernel(first, terms_ref, more_ref, message_ref):
    count, tall, wide = terms_ref.shape
    total = terms_ref[0].astype(F32)
    for k in range(1, count):
        total = total + terms_ref[k].astype(F32)
    if first:
        total = more_ref[...] - total
    total = total.astype(BF16)
    for k in range(count):
        for b in range(wide // LANES):
            at = pl.ds(b * tall, tall)
            message_ref[k, at] = total[:, b * LANES : (b + 1) * LANES]
        if not first:
            message_ref[k, pl.ds(wide // LANES * tall, SCALARS)] = more_ref[...]


def sum_terms(terms, more, first):
    count, tall, wide = terms.shape
    return pl.pallas_call(
        functools.partial(sum_kernel, first),
        out_shape=jax.ShapeDtypeStruct(
            (count, tall * wide // LANES + (0 if first else SCALARS), LANES), BF16
        ),
        compiler_params=pltpu.CompilerParams(vmem_limit_bytes=LITTLE),
        cost_estimate=pl.CostEstimate(
            flops=terms.size, bytes_accessed=4 * terms.size, transcendentals=0
        ),
    )(terms, more)


def back_kernel(first, message_ref, own_ref, other_ref, pieces_ref, sums_ref, errors):
    count = message_ref.shape[0]
    draws, wide = errors.shape[0], errors.shape[1] // count
    rows = own_ref.shape[0]
    for c in range(count):
        for b in range(wide // LANES):
            errors[:, pl.ds(c * wide + b * LANES, LANES)] = message_ref[
                c, pl.ds(b * draws, draws)
            ]
    total = jnp.dot(errors[:, pl.ds(0, rows)], own_ref[...], preferred_element_type=F32)
    total = total + jnp.dot(
        errors[:, pl.ds(rows, rows)], other_ref[...], preferred_element_type=F32
    )
    across = own_ref.shape[1] // LANES
    short = sums_ref.shape[1]
    if first:
        sums_ref[...] = jnp.zeros(sums_ref.shape, F32)
        for m in range(pieces_ref.shape[0]):
            i, j = divmod(m, across)
            piece = total[i * short : (i + 1) * short, j * LANES : (j + 1) * LANES]
            pieces_ref[m] = piece.astype(BF16)
        return
    squares = jnp.zeros((draws, LANES), F32)
    for at in range(0, errors.shape[1], LANES):
        part = errors[:, pl.ds(at, LANES)].astype(F32)
        squares = squares + part * part
    high, low = split(jnp.sum(squares, axis=1, keepdims=True))
    packed = jnp.zeros((SCALARS, LANES), F32)
    for k in range(count):
        part = message_ref[k, pl.ds(wide // LANES * draws, SCALARS)]
        packed = packed + part.astype(F32)
    lane = lane_index(short)
    empty = jnp.zeros((pieces_ref.shape[1] - short - 2, LANES), F32)
    for i in range(sums_ref.shape[0]):
        mine = slice(i * short, (i + 1) * short)
        plain = jnp.zeros((short, LANES), F32)
        for k in range(3):
            line = packed[2 * k : 2 * k + 1] + packed[2 * k + 1 : 2 * k + 2]
            plain = jnp.where(lane == k, row_to_column(line, short, i * short), plain)
        sums_ref[i] = plain
        extra = [column_to_row(high[mine]), column_to_row(low[mine]), empty]
        for j in range(across):
            piece = total[mine, j * LANES : (j + 1) * LANES]
            pieces_ref[i * across + j] = jnp.concatenate([piece] + extra, axis=0).astype(BF16)


def back_terms(message, own, other, draws, pieces, first):
    rows, width = own.shape
    short = draws * width // LANES // pieces
    return pl.pallas_call(
        functools.partial(back_kernel, first),
        in_specs=[IN_VMEM] * 3,
        out_specs=[IN_VMEM] * 2,
        out_shape=[
            jax.ShapeDtypeStruct(
                (pieces, short if first else (short + 17) // 16 * 16, LANES), BF16
            ),
            jax.ShapeDtypeStruct((draws // short, short, LANES), F32),
        ],
        scratch_shapes=[pltpu.VMEM((draws, CORES * rows), BF16)],
        compiler_params=pltpu.CompilerParams(vmem_limit_bytes=MOST),
        cost_estimate=matmul_cost(draws, CORES * rows, width),
    )(message, own, other)


def pick(sums_ref, group_ref, rows):
    mine = sums_ref[group_ref[0]]
    lane = lane_index(rows)
    return [
        jnp.sum(jnp.where(lane == k, mine, 0.0), axis=1, keepdims=True) for k in range(3)
    ]


def add_up(terms_ref):
    total = terms_ref[0].astype(F32)
    for k in range(1, terms_ref.shape[0]):
        total = total + terms_ref[k].astype(F32)
    return total


def received(terms_ref, rows):
    total = add_up(terms_ref)
    norm = row_to_column(total[rows : rows + 1] + total[rows + 1 : rows + 2], rows)
    return total[:rows], norm


def to_all(message_ref, value):
    value = value.astype(BF16)
    for k in range(message_ref.shape[0]):
        message_ref[k] = value


def first_kernel(terms_ref, message_ref, r0_ref):
    r0 = add_up(terms_ref)
    r0_ref[...] = r0
    to_all(message_ref, r0)


def second_kernel(
    group_ref, terms_ref, sums_ref, scale_ref, r0_ref, message_ref, r1_ref, q0_ref, scalar_ref
):
    rows = r0_ref.shape[0]
    product, norm = received(terms_ref, rows)
    rr, weighted, _ = pick(sums_ref, group_ref, rows)
    curve = norm + weighted
    alpha = rr / curve
    q0 = product + scale_ref[...] * r0_ref[...]
    r1 = r0_ref[...] - alpha * q0
    r1_ref[...] = r1
    q0_ref[...] = q0
    scalar_ref[0] = jnp.broadcast_to(rr, (rows, LANES))
    scalar_ref[1] = jnp.broadcast_to(alpha, (rows, LANES))
    scalar_ref[2] = jnp.broadcast_to(curve, (rows, LANES))
    to_all(message_ref, r1)


def third_kernel(
    group_ref, terms_ref, sums_ref, scale_ref, r0_ref, r1_ref, q0_ref, scalar_ref, message_ref
):
    rows = r0_ref.shape[0]
    product, norm = received(terms_ref, rows)
    new, weighted, cross = pick(sums_ref, group_ref, rows)
    rr, alpha0, curve0 = (scalar_ref[k][:, :1] for k in range(3))
    beta = new / rr
    mixed = (cross - new) / alpha0
    curve = norm + weighted + 2.0 * beta * mixed + beta * beta * curve0
    alpha = new / curve
    r1 = r1_ref[...]
    applied = product + scale_ref[...] * r1 + beta * q0_ref[...]
    parts = [r1 - alpha * applied]
    for scalar in (alpha0 + alpha * beta, alpha):
        parts += [column_to_row(part) for part in split(scalar)]
    short = message_ref.shape[1] - rows - 4
    if short > 0:
        parts.append(jnp.zeros((short, LANES), F32))
    to_all(message_ref, jnp.concatenate(parts, axis=0))


def small_call(kernel, group, operands, outs):
    specs = [IN_VMEM] * len(operands)
    if group is not None:
        specs = [pl.BlockSpec(memory_space=pltpu.SMEM)] + specs
        operands = (group,) + operands
    return pl.pallas_call(
        kernel,
        in_specs=specs,
        out_specs=[IN_VMEM] * len(outs),
        out_shape=[jax.ShapeDtypeStruct(shape, kind) for shape, kind in outs],
        compiler_params=pltpu.CompilerParams(vmem_limit_bytes=LITTLE),
        cost_estimate=SMALL,
    )(*operands)


def last_kernel(core_ref, pieces_ref, whole0_ref, whole1_ref, noise_ref, scale_ref, out_ref):
    tall = whole0_ref.shape[1]
    draws = out_ref.shape[1]
    across = out_ref.shape[2] // LANES
    first = pl.multiple_of(core_ref[0] * draws, 8)
    out_ref[0] = noise_ref[pl.ds(first, draws)] * lax.rsqrt(scale_ref[...])
    for m in range(pieces_ref.shape[0]):
        i, j = divmod(m, across)
        at = (pl.ds(i * tall, tall), pl.ds(j * LANES, LANES))
        piece = pieces_ref[m].astype(F32)
        part0, part1 = (
            row_to_column(piece[k : k + 1] + piece[k + 1 : k + 2], tall)
            for k in (tall, tall + 2)
        )
        moved = part0 * whole0_ref[m].astype(F32) + part1 * whole1_ref[m].astype(F32)
        out_ref[(0,) + at] = out_ref[(0,) + at] + moved
        out_ref[(1,) + at] = piece[:tall]


def join_kernel(core_ref, own_ref, other_ref, sampled_ref, residual_ref):
    draws = own_ref.shape[1]
    for core, source in ((core_ref[0], own_ref), (1 - core_ref[0], other_ref)):
        at = pl.ds(pl.multiple_of(core * draws, 8), draws)
        sampled_ref[at] = source[0]
        residual_ref[at] = source[1]


def shards(features, targets, target_noise, prior_noise, precision):
    n_feat = lax.axis_size("feat")
    n_rows = lax.axis_size("rows")
    draws, width = prior_noise.shape
    rows = features.shape[0]
    half = draws // CORES
    chunks = n_feat // CORES
    wide = rows // chunks
    deep = n_rows // CORES
    across = width // LANES
    short = half * across // deep

    levels = [[CORES * z + core for z in range(deep)] for core in range(CORES)]
    swap = [(i, i ^ 1) for i in range(n_rows)]
    other = lax.ppermute(features, "rows", swap)

    scale = precision[None, :]
    line = lax.axis_index("rows").astype(jnp.int32)
    height = line // CORES
    core = (line % CORES).reshape(1)
    group = (height // across).reshape(1)
    place = lax.axis_index("feat")
    first_row = (place % chunks) * wide
    my_targets = lax.dynamic_slice(targets, (first_row,), (wide,))[None, :]
    kept, sent = (
        my_targets + lax.dynamic_slice(target_noise, (side * half, first_row), (half, wide))
        for side in (core[0], 1 - core[0])
    )
    perturbed = jnp.where(place < chunks, kept, lax.ppermute(sent, "rows", swap))
    my_scale = lax.dynamic_slice(precision, ((height % across) * LANES,), (LANES,))[None, :]
    piece, copies = ((short, LANES), F32), ((deep, short, LANES), BF16)

    def over_feat(pieces):
        return lax.all_to_all(pieces, "feat", 0, 0)

    def over_z(pieces):
        return lax.all_to_all(pieces, "rows", 0, 0, axis_index_groups=levels)

    def rest(terms, more, first=False):
        message = sum_terms(over_feat(terms), more, first)
        pieces, sums = back_terms(over_feat(message), features, other, half, deep, first)
        return over_z(pieces), sums

    def apply(vectors):
        return rest(*image_terms(scale, features, other, vectors, n_feat))

    terms, other = first_image_terms(core, prior_noise, scale, features, other, n_feat)
    terms, perturbed, my_scale, group, core = lax.optimization_barrier(
        (terms, perturbed, my_scale, group, core)
    )
    terms, _ = rest(terms, perturbed, True)
    message, r0 = small_call(first_kernel, None, (terms,), (copies, piece))
    whole0 = over_z(message)

    terms, sums = apply((whole0,))
    message, r1, q0, scalars = small_call(
        second_kernel,
        group,
        (terms, sums, my_scale, r0),
        (copies, piece, piece, ((3, short, LANES), F32)),
    )
    whole1 = over_z(message)

    terms, sums = apply((whole1, whole0))
    (message,) = small_call(
        third_kernel,
        group,
        (terms, sums, my_scale, r0, r1, q0, scalars),
        (((deep, (short + 19) // 16 * 16, LANES), BF16),),
    )
    last = (over_z(message), whole0, whole1, prior_noise, scale)
    (mine,) = small_call(last_kernel, core, last, (((2, half, width), F32),))
    full = ((draws, width), F32)
    theirs = lax.ppermute(mine, "rows", swap)
    return tuple(small_call(join_kernel, core, (mine, theirs), (full, full)))


def solution(mesh):
    return jax.shard_map(
        shards,
        mesh=mesh,
        in_specs=(P("rows", "feat"), P("rows"), P(None, "rows"), P(None, "feat"), P("feat")),
        out_specs=(P(None, "feat"), P(None, "feat")),
        check_vma=False,
    )
```

time: 1120 us -> 251 us (0.22)
  waiting for transfers between devices: 968 us -> 1.05 us
  blocking collectives: 94.7 us -> 192 us
  starting transfers between devices: 0.25 us -> 27.3 us
  matrix products: 25.4 us -> 0 us
  Pallas kernels: 0 us -> 23.4 us
  between operations: 14.2 us -> 0.88 us
  other arithmetic: 14.2 us -> 1.99 us
    psum x6 -> x0, waiting for transfers between devices: 968 us -> none  [the longest x3 598 us: back(): return lax.psum(partial_cols, 'rows')]
    all_to_all x0 -> x12, blocking collectives: none -> 192 us  [the longest x6 96.9 us: over_z(): return lax.all_to_all(pieces, 'rows', 0, 0, axis_index_groups=levels)]
    psum x3 -> x0, blocking collectives: 94.7 us -> none  [the longest x2 61.6 us: norms(): return lax.psum(jnp.sum(residual * residual, axis=1), 'feat')]
    ppermute x0 -> x3, starting transfers between devices: none -> 27.3 us  [the longest x1 16.6 us: shards(): theirs = lax.ppermute(mine, 'rows', swap)]
    dot_general x6 -> x0, matrix products: 25.4 us -> none  [the longest x3 16.8 us: image(): jnp.einsum('sd,rd->sr', direction.astype(jnp.bfloat16), features, preferr...]
    pallas_call x0 -> x15, Pallas kernels: none -> 23.4 us  [the longest x2 6.31 us: image_terms(): pl.pallas_call(functools.partial(image_kernel, count), in_specs=[IN_VMEM]...]
  transfers between devices with their start and end apart: 6 -> 3, of which waited for: 6 -> 1; matrix products, arithmetic and copies ran while one was open for 0% -> 1% of each run, Pallas kernels for 0% -> 2%
where the time goes in v1:
time: 251 us; the launch traced here: 250 us
  blocking collectives  192 us (76%)
  starting transfers between devices  27.3 us (11%)
  Pallas kernels  23.4 us (9%)
  local copies, waits for them, and re-layouts  2.92 us (1%)
    all_to_all x6, blocking collectives, over_z(): return lax.all_to_all(pieces, 'rows', 0, 0, axis_index_groups=levels)  96.9 us
    all_to_all x6, blocking collectives, over_feat(): return lax.all_to_all(pieces, 'feat', 0, 0)  95.4 us
    ppermute x1, starting transfers between devices, shards(): theirs = lax.ppermute(mine, 'rows', swap)  16.6 us
    ppermute x1, starting transfers between devices, shards(): other = lax.ppermute(features, 'rows', swap)  8.79 us
    pallas_call x2, Pallas kernels, image_terms(): pl.pallas_call(functools.partial(image_kernel, count), in_specs=[IN_VMEM]...  6.31 us
    pallas_call x3, Pallas kernels, back_terms(): pl.pallas_call(functools.partial(back_kernel, first), in_specs=[IN_VMEM]...  6.22 us
    pallas_call x1, Pallas kernels, first_image_terms(): pl.pallas_call(own_image_kernel, in_specs=[pl.BlockSpec(memory_space=pltp...  5.37 us
  transfers between devices with their start and end apart: 3, of which 1 were waited for; matrix products, arithmetic and copies ran while one was open for 1% of the time, Pallas kernels for 2%

profile of v1, /device:TPU:1, one launch (start us, length us, event | category | flops | bytes accessed | tf_op | source)
XLA Modules:
  0.0 249.9 jit_solution(2258392289797672378)
XLA Ops:
  0.6 8.8 %collective-permute-start = (bf16[5120,512]{1,0:T(8,128)(2,1)}, bf16[5120,512]{1,0:T(8,128)(2,1)}, u32[]{:S(2)}, u32[]{:S(2)}) collective-permute-start(bf16[5120,512]{1,0:T(8,128)(2,1)} %own_ref.9), channel_id=1, source_target_pairs={{0,16},{16,0},{32,48},{48,32},{64,80},{80,64},{96,112},{112,96},{1... | collective-permute-start | bytes 15728648 | tf_op jit(solution)/shard_map/ppermute | solution.py:410
  11.2 1.9 collective-permute-start.1
  13.1 5.4 %shard_map.68 = (bf16[8,48,640]{2,1,0:T(8,128)(2,1)}, bf16[48,512]{1,0:T(8,128)(2,1)}) custom-call(s32[1]{0:T(128)} %bitcast.core_ref, f32[96,512]{1,0:T(8,128)} %noise_ref.3, f32[1,512]{1,0:T(1,128)} %bitcast.7, bf16[5120,512]{1,0:T(8,128)(2,1)} %own_ref.9), custom_call_target="tpu_custom_call" | custom-call | flops 251658240 | bytes 5242880 | tf_op jit(solution)/shard_map/pallas_call | solution.py:143
  18.6 1.1 add_select_fusion.more_ref
  19.7 1.3 copy-done.1
  21.8 3.7 %shard_map.69 = (bf16[16,48,640]{2,1,0:T(8,128)(2,1)S(1)}, bf16[5120,512]{1,0:T(8,128)(2,1)S(1)}) custom-call(bf16[48,512]{1,0:T(8,128)(2,1)S(1)} %copy-done.2, bf16[8,48,640]{2,1,0:T(8,128)(2,1)S(1)} %copy-done.1, bf16[5120,512]{1,0:T(8,128)(2,1)} %collective-permute-done.other_hbm), custom_call_target="tpu_custom_call" | custom-call | flops 251658240 | bytes 5242880 | tf_op jit(solution)/shard_map/pallas_call | solution.py:156
  25.5 18.4 %all_to_all.60.terms_ref = bf16[16,48,640]{2,1,0:T(8,128)(2,1)S(1)} all-to-all(bf16[16,48,640]{2,1,0:T(8,128)(2,1)S(1)} %get-tuple-element.32), channel_id=1, replica_groups=mesh['rows'=32,'feat'=16] {'feat'}, dimensions={0} | all-to-all | bytes 1966080 | tf_op jit(solution)/shard_map/all_to_all | solution.py:429
  44.0 18.5 %all_to_all.61.message_ref = bf16[16,240,128]{2,1,0:T(8,128)(2,1)S(1)} all-to-all(bf16[16,240,128]{2,1,0:T(8,128)(2,1)S(1)} %shard_map.70), channel_id=1, replica_groups=mesh['rows'=32,'feat'=16] {'feat'}, dimensions={0} | all-to-all | bytes 1966080 | tf_op jit(solution)/shard_map/all_to_all | solution.py:429
  62.5 2.4 shard_map.71
  64.9 24.6 %all_to_all.62.terms_ref = bf16[16,12,128]{2,1,0:T(8,128)(2,1)S(1)} all-to-all(bf16[16,12,128]{2,1,0:T(8,128)(2,1)S(1)} %get-tuple-element.34), channel_id=1, replica_groups={{0,32,64,96,128,160,192,224,256,288,320,352,384,416,448,480},{16,48,80,..., dimensions={0} | all-to-all | bytes 98304 | tf_op jit(solution)/shard_map/all_to_all | solution.py:432
  89.5 14.4 %all_to_all.63.refs_0_.refs_1_.whole0_ref = bf16[16,12,128]{2,1,0:T(8,128)(2,1)S(1)} all-to-all(bf16[16,12,128]{2,1,0:T(8,128)(2,1)S(1)} %get-tuple-element.35), channel_id=1, replica_groups={{0,32,64,96,128,160,192,224,256,288,320,352,384,416,448,480},{16,48,80,..., dimensions={0} | all-to-all | bytes 98304 | tf_op jit(solution)/shard_map/all_to_all | solution.py:432
  103.9 3.2 %shard_map.73 = (bf16[16,48,640]{2,1,0:T(8,128)(2,1)S(1)}, bf16[16,128]{1,0:T(8,128)(2,1)S(1)}) custom-call(f32[1,512]{1,0:T(1,128)S(1)} %bitcast.8, bf16[5120,512]{1,0:T(8,128)(2,1)S(1)} %bitcast.6, bf16[5120,512]{1,0:T(8,128)(2,1)S(1)} %get-tuple-element.31.other_ref, bf16[16,12,128]{2,1,0:T(8,128)(2,1)S(1)} %all_to_all.63.refs_0_.refs_1_.whole0_ref), custom_call_target="tpu_custom_call" | custom-call | flops 503316480 | bytes 10485760 | tf_op jit(solution)/shard_map/pallas_call | solution.py:172
  107.0 14.8 %all_to_all.64.terms_ref = bf16[16,48,640]{2,1,0:T(8,128)(2,1)S(1)} all-to-all(bf16[16,48,640]{2,1,0:T(8,128)(2,1)S(1)} %get-tuple-element.36), channel_id=1, replica_groups=mesh['rows'=32,'feat'=16] {'feat'}, dimensions={0} | all-to-all | bytes 1966080 | tf_op jit(solution)/shard_map/all_to_all | solution.py:429
  122.0 14.6 %all_to_all.65.message_ref = bf16[16,256,128]{2,1,0:T(8,128)(2,1)S(1)} all-to-all(bf16[16,256,128]{2,1,0:T(8,128)(2,1)S(1)} %shard_map.74), channel_id=1, replica_groups=mesh['rows'=32,'feat'=16] {'feat'}, dimensions={0} | all-to-all | bytes 2097152 | tf_op jit(solution)/shard_map/all_to_all | solution.py:429
  136.6 1.9 shard_map.75
  138.6 15.3 %all_to_all.66.terms_ref = bf16[16,16,128]{2,1,0:T(8,128)(2,1)S(1)} all-to-all(bf16[16,16,128]{2,1,0:T(8,128)(2,1)S(1)} %get-tuple-element.38), channel_id=1, replica_groups={{0,32,64,96,128,160,192,224,256,288,320,352,384,416,448,480},{16,48,80,..., dimensions={0} | all-to-all | bytes 131072 | tf_op jit(solution)/shard_map/all_to_all | solution.py:432
  154.0 14.2 %all_to_all.67.refs_0_.whole1_ref = bf16[16,12,128]{2,1,0:T(8,128)(2,1)S(1)} all-to-all(bf16[16,12,128]{2,1,0:T(8,128)(2,1)S(1)} %get-tuple-element.42), channel_id=1, replica_groups={{0,32,64,96,128,160,192,224,256,288,320,352,384,416,448,480},{16,48,80,..., dimensions={0} | all-to-all | bytes 98304 | tf_op jit(solution)/shard_map/all_to_all | solution.py:432
  168.2 3.2 %shard_map.77 = (bf16[16,48,640]{2,1,0:T(8,128)(2,1)S(1)}, bf16[16,128]{1,0:T(8,128)(2,1)S(1)}) custom-call(f32[1,512]{1,0:T(1,128)S(1)} %bitcast.9, bf16[5120,512]{1,0:T(8,128)(2,1)S(1)} %bitcast.6, bf16[5120,512]{1,0:T(8,128)(2,1)S(1)} %get-tuple-element.31.other_ref, bf16[16,12,128]{2,1,0:T(8,128)(2,1)S(1)} %all_to_all.67.refs_0_.whole1_ref, ...), custom_call_target="tpu_custom_call" | custom-call | flops 503316480 | bytes 10485760 | tf_op jit(solution)/shard_map/pallas_call | solution.py:172
  171.4 14.1 %all_to_all.68.terms_ref = bf16[16,48,640]{2,1,0:T(8,128)(2,1)S(1)} all-to-all(bf16[16,48,640]{2,1,0:T(8,128)(2,1)S(1)} %get-tuple-element.43), channel_id=1, replica_groups=mesh['rows'=32,'feat'=16] {'feat'}, dimensions={0} | all-to-all | bytes 1966080 | tf_op jit(solution)/shard_map/all_to_all | solution.py:429
  185.7 15.1 %all_to_all.69.message_ref = bf16[16,256,128]{2,1,0:T(8,128)(2,1)S(1)} all-to-all(bf16[16,256,128]{2,1,0:T(8,128)(2,1)S(1)} %shard_map.78), channel_id=1, replica_groups=mesh['rows'=32,'feat'=16] {'feat'}, dimensions={0} | all-to-all | bytes 2097152 | tf_op jit(solution)/shard_map/all_to_all | solution.py:429
  200.7 1.9 shard_map.79
  202.7 14.2 %all_to_all.70.terms_ref = bf16[16,16,128]{2,1,0:T(8,128)(2,1)S(1)} all-to-all(bf16[16,16,128]{2,1,0:T(8,128)(2,1)S(1)} %get-tuple-element.45), channel_id=1, replica_groups={{0,32,64,96,128,160,192,224,256,288,320,352,384,416,448,480},{16,48,80,..., dimensions={0} | all-to-all | bytes 131072 | tf_op jit(solution)/shard_map/all_to_all | solution.py:432
  217.1 14.2 %all_to_all.71.pieces_ref = bf16[16,16,128]{2,1,0:T(8,128)(2,1)S(1)} all-to-all(bf16[16,16,128]{2,1,0:T(8,128)(2,1)S(1)} %shard_map.80), channel_id=1, replica_groups={{0,32,64,96,128,160,192,224,256,288,320,352,384,416,448,480},{16,48,80,..., dimensions={0} | all-to-all | bytes 131072 | tf_op jit(solution)/shard_map/all_to_all | solution.py:432
  231.4 16.6 %collective-permute-start.2 = (f32[2,48,512]{2,1,0:T(8,128)S(1)}, f32[2,48,512]{2,1,0:T(8,128)S(1)}, u32[]{:S(2)}, u32[]{:S(2)}) collective-permute-start(f32[2,48,512]{2,1,0:T(8,128)S(1)} %shard_map.81.own_ref), channel_id=1, source_target_pairs={{0,16},{16,0},{32,48},{48,32},{64,80},{80,64},{96,112},{112,96},{1... | collective-permute-start | bytes 589832 | tf_op jit(solution)/shard_map/ppermute | solution.py:469
  (26 shorter events, 5.4 us)
Async XLA Ops:
  0.6 17.9 %copy-start.3 = (f32[512]{0:T(512)S(1)}, f32[512]{0:T(512)}, u32[]{:S(2)}) copy-start(f32[512]{0:T(512)} %param.9) | copy-start | bytes 6148
  0.6 19.1 %collective-permute-start = (bf16[5120,512]{1,0:T(8,128)(2,1)}, bf16[5120,512]{1,0:T(8,128)(2,1)}, u32[]{:S(2)}, u32[]{:S(2)}) collective-permute-start(bf16[5120,512]{1,0:T(8,128)(2,1)} %own_ref.9), channel_id=1, source_target_pairs={{0,16},{16,0},{32,48},{48,32},{64,80},{80,64},{96,112},{112,96},{1... | collective-permute-start | bytes 15728648 | tf_op jit(solution)/shard_map/ppermute | solution.py:410
  11.2 7.5 %collective-permute-start.1 = (f32[48,640]{1,0:T(8,128)S(1)}, f32[48,640]{1,0:T(8,128)S(1)}, u32[]{:S(2)}, u32[]{:S(2)}) collective-permute-start(f32[48,640]{1,0:T(8,128)S(1)} %dynamic-slice_add_fusion), channel_id=1, source_target_pairs={{0,16},{16,0},{32,48},{48,32},{64,80},{80,64},{96,112},{112,96},{1... | collective-permute-start | bytes 368648 | tf_op jit(solution)/shard_map/ppermute | solution.py:424
  18.6 43.9 %slice-start = ((s8[5242880]{0:T(1024)(128)(4,1)}), s8[4194304]{0:T(1024)(128)(4,1)S(1)}, s32[]{:S(2)}) async-start(s8[5242880]{0:T(1024)(128)(4,1)} %bitcast.5), calls=%async_computation.12 | async-start | bytes 8388608
  19.7 1.3 copy-start.1
  21.0 0.8 copy-start.2
  21.8 40.7 %slice-start.1 = ((s8[5242880]{0:T(1024)(128)(4,1)}), s8[1048576]{0:T(1024)(128)(4,1)S(1)}, s32[]{:S(2)}) async-start(s8[5242880]{0:T(1024)(128)(4,1)} %bitcast.5), calls=%async_computation.13 | async-start | bytes 2097152
  200.7 30.5 %copy-start = (f32[96,512]{1,0:T(8,128)S(1)}, f32[96,512]{1,0:T(8,128)}, u32[]{:S(2)}) copy-start(f32[96,512]{1,0:T(8,128)} %noise_ref.3) | copy-start | bytes 589828
  231.4 17.7 %collective-permute-start.2 = (f32[2,48,512]{2,1,0:T(8,128)S(1)}, f32[2,48,512]{2,1,0:T(8,128)S(1)}, u32[]{:S(2)}, u32[]{:S(2)}) collective-permute-start(f32[2,48,512]{2,1,0:T(8,128)S(1)} %shard_map.81.own_ref), channel_id=1, source_target_pairs={{0,16},{16,0},{32,48},{48,32},{64,80},{80,64},{96,112},{112,96},{1... | collective-permute-start | bytes 589832 | tf_op jit(solution)/shard_map/ppermute | solution.py:469

commit v2 on v1

--- a/solution.py
+++ b/solution.py
@@ -10,10 +10,9 @@
 
 CORES = 2
 LANES = 128
-BLOCKS = 4
+BLOCKS = 8
 F32, BF16 = jnp.float32, jnp.bfloat16
 MOST = 16 * 2**20
-WHOLE = 56 * 2**20
 SCALARS = 16
 LITTLE = 8 * 2**20
 IN_VMEM = pl.BlockSpec(memory_space=pltpu.VMEM)
@@ -84,15 +83,12 @@
     multiply_out(value, f_ref, store, pieces_ref.shape[2], copies)
 
 
-def own_image_kernel(
-    core_ref, noise_ref, scale_ref, own_hbm, pieces_ref, value_ref, kept_ref, sems
-):
-    copies = fetch(own_hbm, kept_ref, sems)
+def own_image_kernel(core_ref, noise_ref, scale_ref, own_ref, pieces_ref, value_ref):
     draws = pieces_ref.shape[1]
     first = pl.multiple_of(core_ref[0] * draws, 8)
     value = (noise_ref[pl.ds(first, draws)] * lax.rsqrt(scale_ref[...])).astype(BF16)
     value_ref[...] = value
-    multiply_into(value, kept_ref, pieces_ref, 0, copies)
+    multiply_into(value, own_ref, pieces_ref, 0)
 
 
 def other_image_kernel(value_ref, half_ref, other_hbm, pieces_ref, kept_ref, sems):
@@ -136,29 +132,27 @@
     rows, width = own.shape
     draws = noise.shape[0] // CORES
     shape = (n_feat // CORES, draws, CORES * rows // n_feat)
-    anywhere = [pl.BlockSpec(memory_space=pl.ANY)]
-    kept = jax.ShapeDtypeStruct((rows, width), BF16)
-    sems = [pltpu.SemaphoreType.DMA((math.gcd(shape[0], BLOCKS),))]
-    params = pltpu.CompilerParams(vmem_limit_bytes=WHOLE)
+    params = pltpu.CompilerParams(vmem_limit_bytes=MOST)
     half, value = pl.pallas_call(
         own_image_kernel,
-        in_specs=[pl.BlockSpec(memory_space=pltpu.SMEM)] + [IN_VMEM] * 2 + anywhere,
+        in_specs=[pl.BlockSpec(memory_space=pltpu.SMEM)] + [IN_VMEM] * 3,
         out_specs=[IN_VMEM] * 2,
         out_shape=[
             jax.ShapeDtypeStruct(shape, BF16),
             jax.ShapeDtypeStruct((draws, width), BF16),
         ],
-        scratch_shapes=[pltpu.VMEM((rows, width), BF16)] + sems,
         compiler_params=params,
         cost_estimate=matmul_cost(draws, rows, width),
     )(core, noise, scale, own)
-    params = pltpu.CompilerParams(vmem_limit_bytes=MOST)
     terms, other = pl.pallas_call(
         other_image_kernel,
-        in_specs=[IN_VMEM] * 2 + anywhere,
+        in_specs=[IN_VMEM] * 2 + [pl.BlockSpec(memory_space=pl.ANY)],
         out_specs=[IN_VMEM] * 2,
-        out_shape=[jax.ShapeDtypeStruct((n_feat,) + shape[1:], BF16), kept],
-        scratch_shapes=sems,
+        out_shape=[
+            jax.ShapeDtypeStruct((n_feat,) + shape[1:], BF16),
+            jax.ShapeDtypeStruct((rows, width), BF16),
+        ],
+        scratch_shapes=[pltpu.SemaphoreType.DMA((math.gcd(shape[0], BLOCKS),))],
         compiler_params=params,
         cost_estimate=matmul_cost(draws, rows, width),
     )(value, half, other)

time: 251 us -> 249 us (level)
  Pallas kernels: 23.4 us -> 20.1 us
    pallas_call x1, Pallas kernels: 5.37 us -> 1.62 us  [first_image_terms(): pl.pallas_call(own_image_kernel, in_specs=[pl.BlockSpec(memory_space=pltp...]
  transfers between devices with their start and end apart: 3 -> 3, of which waited for: 1 -> 1; matrix products, arithmetic and copies ran while one was open for 1% -> 1% of each run, Pallas kernels for 2% -> 1%
where the time goes in v2:
time: 249 us
  blocking collectives  192 us (77%)
  starting transfers between devices  27.3 us (11%)
  Pallas kernels  20.1 us (8%)
  local copies, waits for them, and re-layouts  4.96 us (2%)
    all_to_all x6, blocking collectives, over_z(): return lax.all_to_all(pieces, 'rows', 0, 0, axis_index_groups=levels)  96.9 us
    all_to_all x6, blocking collectives, over_feat(): return lax.all_to_all(pieces, 'feat', 0, 0)  95.4 us
    ppermute x1, starting transfers between devices, shards(): theirs = lax.ppermute(mine, 'rows', swap)  16.6 us
    ppermute x1, starting transfers between devices, shards(): other = lax.ppermute(features, 'rows', swap)  8.79 us
    pallas_call x2, Pallas kernels, image_terms(): pl.pallas_call(functools.partial(image_kernel, count), in_specs=[IN_VMEM]...  6.3 us
    pallas_call x3, Pallas kernels, back_terms(): pl.pallas_call(functools.partial(back_kernel, first), in_specs=[IN_VMEM]...  6.21 us
  transfers between devices with their start and end apart: 3, of which 1 were waited for; matrix products, arithmetic and copies ran while one was open for 1% of the time, Pallas kernels for 1%

profile of v2, /device:TPU:1, one launch (start us, length us, event | category | flops | bytes accessed | tf_op | source)
XLA Modules:
  0.0 248.6 jit_solution(6271380971001353833)
XLA Ops:
  0.6 8.8 %collective-permute-start = (bf16[5120,512]{1,0:T(8,128)(2,1)}, bf16[5120,512]{1,0:T(8,128)(2,1)}, u32[]{:S(2)}, u32[]{:S(2)}) collective-permute-start(bf16[5120,512]{1,0:T(8,128)(2,1)} %own_ref.11), channel_id=1, source_target_pairs={{0,16},{16,0},{32,48},{48,32},{64,80},{80,64},{96,112},{112,96},{1... | collective-permute-start | bytes 15728648 | tf_op jit(solution)/shard_map/ppermute | solution.py:404
  11.2 1.9 collective-permute-start.1
  13.1 2.5 copy-done
  17.2 1.6 shard_map.68
  19.0 1.1 add_select_fusion.more_ref
  20.1 4.2 %shard_map.69 = (bf16[16,48,640]{2,1,0:T(8,128)(2,1)S(1)}, bf16[5120,512]{1,0:T(8,128)(2,1)S(1)}) custom-call(bf16[48,512]{1,0:T(8,128)(2,1)S(1)} %get-tuple-element.26.value_ref, bf16[8,48,640]{2,1,0:T(8,128)(2,1)S(1)} %get-tuple-element.27.half_ref, bf16[5120,512]{1,0:T(8,128)(2,1)} %collective-permute-done.other_hbm), custom_call_target="tpu_custom_call" | custom-call | flops 251658240 | bytes 5242880 | tf_op jit(solution)/shard_map/pallas_call | solution.py:147
  24.2 18.4 %all_to_all.60.terms_ref = bf16[16,48,640]{2,1,0:T(8,128)(2,1)S(1)} all-to-all(bf16[16,48,640]{2,1,0:T(8,128)(2,1)S(1)} %get-tuple-element.32), channel_id=1, replica_groups=mesh['rows'=32,'feat'=16] {'feat'}, dimensions={0} | all-to-all | bytes 1966080 | tf_op jit(solution)/shard_map/all_to_all | solution.py:423
  42.8 18.5 %all_to_all.61.message_ref = bf16[16,240,128]{2,1,0:T(8,128)(2,1)S(1)} all-to-all(bf16[16,240,128]{2,1,0:T(8,128)(2,1)S(1)} %shard_map.70), channel_id=1, replica_groups=mesh['rows'=32,'feat'=16] {'feat'}, dimensions={0} | all-to-all | bytes 1966080 | tf_op jit(solution)/shard_map/all_to_all | solution.py:423
  61.2 2.4 shard_map.71
  63.6 24.6 %all_to_all.62.terms_ref = bf16[16,12,128]{2,1,0:T(8,128)(2,1)S(1)} all-to-all(bf16[16,12,128]{2,1,0:T(8,128)(2,1)S(1)} %get-tuple-element.34), channel_id=1, replica_groups={{0,32,64,96,128,160,192,224,256,288,320,352,384,416,448,480},{16,48,80,..., dimensions={0} | all-to-all | bytes 98304 | tf_op jit(solution)/shard_map/all_to_all | solution.py:426
  88.2 14.4 %all_to_all.63.refs_0_.refs_1_.whole0_ref = bf16[16,12,128]{2,1,0:T(8,128)(2,1)S(1)} all-to-all(bf16[16,12,128]{2,1,0:T(8,128)(2,1)S(1)} %get-tuple-element.35), channel_id=1, replica_groups={{0,32,64,96,128,160,192,224,256,288,320,352,384,416,448,480},{16,48,80,..., dimensions={0} | all-to-all | bytes 98304 | tf_op jit(solution)/shard_map/all_to_all | solution.py:426
  102.6 3.1 %shard_map.73 = (bf16[16,48,640]{2,1,0:T(8,128)(2,1)S(1)}, bf16[16,128]{1,0:T(8,128)(2,1)S(1)}) custom-call(f32[1,512]{1,0:T(1,128)S(1)} %bitcast.8, bf16[5120,512]{1,0:T(8,128)(2,1)S(1)} %bitcast.6, bf16[5120,512]{1,0:T(8,128)(2,1)S(1)} %get-tuple-element.31.other_ref, bf16[16,12,128]{2,1,0:T(8,128)(2,1)S(1)} %all_to_all.63.refs_0_.refs_1_.whole0_ref), custom_call_target="tpu_custom_call" | custom-call | flops 503316480 | bytes 10485760 | tf_op jit(solution)/shard_map/pallas_call | solution.py:166
  105.8 14.8 %all_to_all.64.terms_ref = bf16[16,48,640]{2,1,0:T(8,128)(2,1)S(1)} all-to-all(bf16[16,48,640]{2,1,0:T(8,128)(2,1)S(1)} %get-tuple-element.36), channel_id=1, replica_groups=mesh['rows'=32,'feat'=16] {'feat'}, dimensions={0} | all-to-all | bytes 1966080 | tf_op jit(solution)/shard_map/all_to_all | solution.py:423
  120.7 14.6 %all_to_all.65.message_ref = bf16[16,256,128]{2,1,0:T(8,128)(2,1)S(1)} all-to-all(bf16[16,256,128]{2,1,0:T(8,128)(2,1)S(1)} %shard_map.74), channel_id=1, replica_groups=mesh['rows'=32,'feat'=16] {'feat'}, dimensions={0} | all-to-all | bytes 2097152 | tf_op jit(solution)/shard_map/all_to_all | solution.py:423
  135.3 1.9 shard_map.75
  137.3 15.3 %all_to_all.66.terms_ref = bf16[16,16,128]{2,1,0:T(8,128)(2,1)S(1)} all-to-all(bf16[16,16,128]{2,1,0:T(8,128)(2,1)S(1)} %get-tuple-element.38), channel_id=1, replica_groups={{0,32,64,96,128,160,192,224,256,288,320,352,384,416,448,480},{16,48,80,..., dimensions={0} | all-to-all | bytes 131072 | tf_op jit(solution)/shard_map/all_to_all | solution.py:426
  152.7 14.2 %all_to_all.67.refs_0_.whole1_ref = bf16[16,12,128]{2,1,0:T(8,128)(2,1)S(1)} all-to-all(bf16[16,12,128]{2,1,0:T(8,128)(2,1)S(1)} %get-tuple-element.42), channel_id=1, replica_groups={{0,32,64,96,128,160,192,224,256,288,320,352,384,416,448,480},{16,48,80,..., dimensions={0} | all-to-all | bytes 98304 | tf_op jit(solution)/shard_map/all_to_all | solution.py:426
  166.9 3.2 %shard_map.77 = (bf16[16,48,640]{2,1,0:T(8,128)(2,1)S(1)}, bf16[16,128]{1,0:T(8,128)(2,1)S(1)}) custom-call(f32[1,512]{1,0:T(1,128)S(1)} %bitcast.9, bf16[5120,512]{1,0:T(8,128)(2,1)S(1)} %bitcast.6, bf16[5120,512]{1,0:T(8,128)(2,1)S(1)} %get-tuple-element.31.other_ref, bf16[16,12,128]{2,1,0:T(8,128)(2,1)S(1)} %all_to_all.67.refs_0_.whole1_ref, ...), custom_call_target="tpu_custom_call" | custom-call | flops 503316480 | bytes 10485760 | tf_op jit(solution)/shard_map/pallas_call | solution.py:166
  170.1 14.1 %all_to_all.68.terms_ref = bf16[16,48,640]{2,1,0:T(8,128)(2,1)S(1)} all-to-all(bf16[16,48,640]{2,1,0:T(8,128)(2,1)S(1)} %get-tuple-element.43), channel_id=1, replica_groups=mesh['rows'=32,'feat'=16] {'feat'}, dimensions={0} | all-to-all | bytes 1966080 | tf_op jit(solution)/shard_map/all_to_all | solution.py:423
  184.4 15.1 %all_to_all.69.message_ref = bf16[16,256,128]{2,1,0:T(8,128)(2,1)S(1)} all-to-all(bf16[16,256,128]{2,1,0:T(8,128)(2,1)S(1)} %shard_map.78), channel_id=1, replica_groups=mesh['rows'=32,'feat'=16] {'feat'}, dimensions={0} | all-to-all | bytes 2097152 | tf_op jit(solution)/shard_map/all_to_all | solution.py:423
  199.5 1.9 shard_map.79
  201.4 14.2 %all_to_all.70.terms_ref = bf16[16,16,128]{2,1,0:T(8,128)(2,1)S(1)} all-to-all(bf16[16,16,128]{2,1,0:T(8,128)(2,1)S(1)} %get-tuple-element.45), channel_id=1, replica_groups={{0,32,64,96,128,160,192,224,256,288,320,352,384,416,448,480},{16,48,80,..., dimensions={0} | all-to-all | bytes 131072 | tf_op jit(solution)/shard_map/all_to_all | solution.py:426
  215.8 14.2 %all_to_all.71.pieces_ref = bf16[16,16,128]{2,1,0:T(8,128)(2,1)S(1)} all-to-all(bf16[16,16,128]{2,1,0:T(8,128)(2,1)S(1)} %shard_map.80), channel_id=1, replica_groups={{0,32,64,96,128,160,192,224,256,288,320,352,384,416,448,480},{16,48,80,..., dimensions={0} | all-to-all | bytes 131072 | tf_op jit(solution)/shard_map/all_to_all | solution.py:426
  230.1 16.6 %collective-permute-start.2 = (f32[2,48,512]{2,1,0:T(8,128)S(1)}, f32[2,48,512]{2,1,0:T(8,128)S(1)}, u32[]{:S(2)}, u32[]{:S(2)}) collective-permute-start(f32[2,48,512]{2,1,0:T(8,128)S(1)} %shard_map.81.own_ref), channel_id=1, source_target_pairs={{0,16},{16,0},{32,48},{48,32},{64,80},{80,64},{96,112},{112,96},{1... | collective-permute-start | bytes 589832 | tf_op jit(solution)/shard_map/ppermute | solution.py:463
  (28 shorter events, 6.2 us)
Async XLA Ops:
  0.6 18.2 %copy-start.4 = (f32[512]{0:T(512)S(1)}, f32[512]{0:T(512)}, u32[]{:S(2)}) copy-start(f32[512]{0:T(512)} %param.9) | copy-start | bytes 6148
  0.6 19.4 %collective-permute-start = (bf16[5120,512]{1,0:T(8,128)(2,1)}, bf16[5120,512]{1,0:T(8,128)(2,1)}, u32[]{:S(2)}, u32[]{:S(2)}) collective-permute-start(bf16[5120,512]{1,0:T(8,128)(2,1)} %own_ref.11), channel_id=1, source_target_pairs={{0,16},{16,0},{32,48},{48,32},{64,80},{80,64},{96,112},{112,96},{1... | collective-permute-start | bytes 15728648 | tf_op jit(solution)/shard_map/ppermute | solution.py:404
  11.2 7.8 %collective-permute-start.1 = (f32[48,640]{1,0:T(8,128)S(1)}, f32[48,640]{1,0:T(8,128)S(1)}, u32[]{:S(2)}, u32[]{:S(2)}) collective-permute-start(f32[48,640]{1,0:T(8,128)S(1)} %dynamic-slice_add_fusion), channel_id=1, source_target_pairs={{0,16},{16,0},{32,48},{48,32},{64,80},{80,64},{96,112},{112,96},{1... | collective-permute-start | bytes 368648 | tf_op jit(solution)/shard_map/ppermute | solution.py:418
  13.1 2.5 %copy-start = (bf16[5120,512]{1,0:T(8,128)(2,1)S(1)}, bf16[5120,512]{1,0:T(8,128)(2,1)}, u32[]{:S(2)}) copy-start(bf16[5120,512]{1,0:T(8,128)(2,1)} %own_ref.11) | copy-start | bytes 15728644
  15.6 0.9 copy-start.1
  16.5 0.7 copy-start.3
  19.0 42.3 %slice-start = ((s8[5242880]{0:T(1024)(128)(4,1)}), s8[4194304]{0:T(1024)(128)(4,1)S(1)}, s32[]{:S(2)}) async-start(s8[5242880]{0:T(1024)(128)(4,1)} %bitcast.5), calls=%async_computation.12 | async-start | bytes 8388608
  20.0 41.2 %slice-start.1 = ((s8[5242880]{0:T(1024)(128)(4,1)}), s8[1048576]{0:T(1024)(128)(4,1)S(1)}, s32[]{:S(2)}) async-start(s8[5242880]{0:T(1024)(128)(4,1)} %bitcast.5), calls=%async_computation.13 | async-start | bytes 2097152
  199.5 30.5 %copy-start.2 = (f32[96,512]{1,0:T(8,128)S(1)}, f32[96,512]{1,0:T(8,128)}, u32[]{:S(2)}) copy-start(f32[96,512]{1,0:T(8,128)} %noise_ref.3) | copy-start | bytes 589828
  230.1 17.7 %collective-permute-start.2 = (f32[2,48,512]{2,1,0:T(8,128)S(1)}, f32[2,48,512]{2,1,0:T(8,128)S(1)}, u32[]{:S(2)}, u32[]{:S(2)}) collective-permute-start(f32[2,48,512]{2,1,0:T(8,128)S(1)} %shard_map.81.own_ref), channel_id=1, source_target_pairs={{0,16},{16,0},{32,48},{48,32},{64,80},{80,64},{96,112},{112,96},{1... | collective-permute-start | bytes 589832 | tf_op jit(solution)/shard_map/ppermute | solution.py:463

commit v3 on v2

--- a/solution.py
+++ b/solution.py
@@ -11,6 +11,7 @@
 CORES = 2
 LANES = 128
 BLOCKS = 8
+PARTS = 4
 F32, BF16 = jnp.float32, jnp.bfloat16
 MOST = 16 * 2**20
 SCALARS = 16
@@ -49,7 +50,7 @@
 
 def multiply_out(value, f_ref, store, wide, copies=None):
     chunks = f_ref.shape[0] // wide
-    blocks = math.gcd(chunks, BLOCKS)
+    blocks = math.gcd(chunks, BLOCKS if copies is None else PARTS)
     per = chunks // blocks
     size = per * wide
     for k in range(blocks):
@@ -152,7 +153,7 @@
             jax.ShapeDtypeStruct((n_feat,) + shape[1:], BF16),
             jax.ShapeDtypeStruct((rows, width), BF16),
         ],
-        scratch_shapes=[pltpu.SemaphoreType.DMA((math.gcd(shape[0], BLOCKS),))],
+        scratch_shapes=[pltpu.SemaphoreType.DMA((math.gcd(shape[0], PARTS),))],
         compiler_params=params,
         cost_estimate=matmul_cost(draws, rows, width),
     )(value, half, other)
@@ -177,13 +178,19 @@
     )(scale, own, other, *vectors)
 
 
-def sum_kernel(first, terms_ref, more_ref, message_ref):
+def sum_kernel(first, *refs):
+    terms_ref, message_ref = refs[0], refs[-1]
     count, tall, wide = terms_ref.shape
     total = terms_ref[0].astype(F32)
     for k in range(1, count):
         total = total + terms_ref[k].astype(F32)
     if first:
-        total = more_ref[...] - total
+        kept_ref, received_ref, core_ref, far_ref = refs[1:5]
+        mine = pl.ds(pl.multiple_of(core_ref[0] * tall, 8), tall)
+        is_kept = jnp.full((tall, wide), far_ref[0]) == 0
+        total = jnp.where(is_kept, kept_ref[mine], received_ref[mine]) - total
+    else:
+        more_ref = refs[1]
     total = total.astype(BF16)
     for k in range(count):
         for b in range(wide // LANES):
@@ -193,10 +200,16 @@
             message_ref[k, pl.ds(wide // LANES * tall, SCALARS)] = more_ref[...]
 
 
-def sum_terms(terms, more, first):
+def sum_terms(terms, more):
+    first = len(more) > 1
     count, tall, wide = terms.shape
+    specs = [IN_VMEM] * (1 + len(more))
+    if first:
+        specs[-2:] = [pl.BlockSpec(memory_space=pltpu.SMEM)] * 2
     return pl.pallas_call(
         functools.partial(sum_kernel, first),
+        in_specs=specs,
+        out_specs=IN_VMEM,
         out_shape=jax.ShapeDtypeStruct(
             (count, tall * wide // LANES + (0 if first else SCALARS), LANES), BF16
         ),
@@ -204,7 +217,7 @@
         cost_estimate=pl.CostEstimate(
             flops=terms.size, bytes_accessed=4 * terms.size, transcendentals=0
         ),
-    )(terms, more)
+    )(terms, *more)
 
 
 def back_kernel(first, message_ref, own_ref, other_ref, pieces_ref, sums_ref, errors):
@@ -410,12 +423,11 @@
     group = (height // across).reshape(1)
     place = lax.axis_index("feat")
     first_row = (place % chunks) * wide
-    my_targets = lax.dynamic_slice(targets, (first_row,), (wide,))[None, :]
-    kept, sent = (
-        my_targets + lax.dynamic_slice(target_noise, (side * half, first_row), (half, wide))
-        for side in (core[0], 1 - core[0])
-    )
-    perturbed = jnp.where(place < chunks, kept, lax.ppermute(sent, "rows", swap))
+    perturbed = lax.dynamic_slice(targets, (first_row,), (wide,))[None, :] + lax.dynamic_slice(
+        target_noise, (0, first_row), (draws, wide)
+    )
+    received = lax.ppermute(perturbed, "rows", swap)
+    far = (place >= chunks).astype(jnp.int32).reshape(1)
     my_scale = lax.dynamic_slice(precision, ((height % across) * LANES,), (LANES,))[None, :]
     piece, copies = ((short, LANES), F32), ((deep, short, LANES), BF16)
 
@@ -426,18 +438,19 @@
         return lax.all_to_all(pieces, "rows", 0, 0, axis_index_groups=levels)
 
     def rest(terms, more, first=False):
-        message = sum_terms(over_feat(terms), more, first)
+        message = sum_terms(over_feat(terms), more)
         pieces, sums = back_terms(over_feat(message), features, other, half, deep, first)
         return over_z(pieces), sums
 
     def apply(vectors):
-        return rest(*image_terms(scale, features, other, vectors, n_feat))
+        terms, sums = image_terms(scale, features, other, vectors, n_feat)
+        return rest(terms, (sums,))
 
     terms, other = first_image_terms(core, prior_noise, scale, features, other, n_feat)
-    terms, perturbed, my_scale, group, core = lax.optimization_barrier(
-        (terms, perturbed, my_scale, group, core)
-    )
-    terms, _ = rest(terms, perturbed, True)
+    terms, perturbed, received, far, my_scale, group, core = lax.optimization_barrier(
+        (terms, perturbed, received, far, my_scale, group, core)
+    )
+    terms, _ = rest(terms, (perturbed, received, core, far), True)
     message, r0 = small_call(first_kernel, None, (terms,), (copies, piece))
     whole0 = over_z(message)
 

time: 249 us -> 248 us (level)
  transfers between devices with their start and end apart: 3 -> 3, of which waited for: 1 -> 1; matrix products, arithmetic and copies ran while one was open for 1% -> 1% of each run, Pallas kernels for 1% -> 2%
where the time goes in v3:
time: 248 us; the launch traced here: 247 us
  blocking collectives  192 us (77%)
  starting transfers between devices  27.3 us (11%)
  Pallas kernels  19.7 us (8%)
  local copies, waits for them, and re-layouts  4.96 us (2%)
    all_to_all x6, blocking collectives, over_z(): return lax.all_to_all(pieces, 'rows', 0, 0, axis_index_groups=levels)  96.9 us
    all_to_all x6, blocking collectives, over_feat(): return lax.all_to_all(pieces, 'feat', 0, 0)  95.4 us
    ppermute x1, starting transfers between devices, shards(): theirs = lax.ppermute(mine, 'rows', swap)  16.6 us
    ppermute x1, starting transfers between devices, shards(): other = lax.ppermute(features, 'rows', swap)  8.79 us
    pallas_call x2, Pallas kernels, image_terms(): pl.pallas_call(functools.partial(image_kernel, count), in_specs=[IN_VMEM]...  6.31 us
    pallas_call x3, Pallas kernels, back_terms(): pl.pallas_call(functools.partial(back_kernel, first), in_specs=[IN_VMEM]...  6.22 us
  transfers between devices with their start and end apart: 3, of which 1 were waited for; matrix products, arithmetic and copies ran while one was open for 1% of the time, Pallas kernels for 2%

profile of v3, /device:TPU:1, one launch (start us, length us, event | category | flops | bytes accessed | tf_op | source)
XLA Modules:
  0.0 247.1 jit_solution(3552925253322002699)
XLA Ops:
  0.6 8.8 %collective-permute-start = (bf16[5120,512]{1,0:T(8,128)(2,1)}, bf16[5120,512]{1,0:T(8,128)(2,1)}, u32[]{:S(2)}, u32[]{:S(2)}) collective-permute-start(bf16[5120,512]{1,0:T(8,128)(2,1)} %own_ref.11), channel_id=1, source_target_pairs={{0,16},{16,0},{32,48},{48,32},{64,80},{80,64},{96,112},{112,96},{1... | collective-permute-start | bytes 15728648 | tf_op jit(solution)/shard_map/ppermute | solution.py:417
  11.2 1.9 collective-permute-start.1
  13.2 2.5 %copy-done = bf16[5120,512]{1,0:T(8,128)(2,1)S(1)} copy-done((bf16[5120,512]{1,0:T(8,128)(2,1)S(1)}, bf16[5120,512]{1,0:T(8,128)(2,1)}, u32[]{:S(2)}) %copy-start) | copy-done | bytes 5242904
  17.3 1.6 shard_map.68
  19.0 3.7 %shard_map.69 = (bf16[16,48,640]{2,1,0:T(8,128)(2,1)S(1)}, bf16[5120,512]{1,0:T(8,128)(2,1)S(1)}) custom-call(bf16[48,512]{1,0:T(8,128)(2,1)S(1)} %get-tuple-element.28.value_ref, bf16[8,48,640]{2,1,0:T(8,128)(2,1)S(1)} %get-tuple-element.29.half_ref, bf16[5120,512]{1,0:T(8,128)(2,1)} %collective-permute-done.other_hbm), custom_call_target="tpu_custom_call" | custom-call | flops 251658240 | bytes 5242880 | tf_op jit(solution)/shard_map/pallas_call | solution.py:148
  22.7 18.4 %all_to_all.60.refs_0_ = bf16[16,48,640]{2,1,0:T(8,128)(2,1)S(1)} all-to-all(bf16[16,48,640]{2,1,0:T(8,128)(2,1)S(1)} %get-tuple-element.34), channel_id=1, replica_groups=mesh['rows'=32,'feat'=16] {'feat'}, dimensions={0} | all-to-all | bytes 1966080 | tf_op jit(solution)/shard_map/all_to_all | solution.py:435
  41.3 18.5 %all_to_all.61.message_ref = bf16[16,240,128]{2,1,0:T(8,128)(2,1)S(1)} all-to-all(bf16[16,240,128]{2,1,0:T(8,128)(2,1)S(1)} %shard_map.70), channel_id=1, replica_groups=mesh['rows'=32,'feat'=16] {'feat'}, dimensions={0} | all-to-all | bytes 1966080 | tf_op jit(solution)/shard_map/all_to_all | solution.py:435
  59.7 2.4 shard_map.71
  62.1 24.6 %all_to_all.62.terms_ref = bf16[16,12,128]{2,1,0:T(8,128)(2,1)S(1)} all-to-all(bf16[16,12,128]{2,1,0:T(8,128)(2,1)S(1)} %get-tuple-element.38), channel_id=1, replica_groups={{0,32,64,96,128,160,192,224,256,288,320,352,384,416,448,480},{16,48,80,..., dimensions={0} | all-to-all | bytes 98304 | tf_op jit(solution)/shard_map/all_to_all | solution.py:438
  86.7 14.4 %all_to_all.63.refs_0_.refs_1_.whole0_ref = bf16[16,12,128]{2,1,0:T(8,128)(2,1)S(1)} all-to-all(bf16[16,12,128]{2,1,0:T(8,128)(2,1)S(1)} %get-tuple-element.39), channel_id=1, replica_groups={{0,32,64,96,128,160,192,224,256,288,320,352,384,416,448,480},{16,48,80,..., dimensions={0} | all-to-all | bytes 98304 | tf_op jit(solution)/shard_map/all_to_all | solution.py:438
  101.1 3.2 %shard_map.73 = (bf16[16,48,640]{2,1,0:T(8,128)(2,1)S(1)}, bf16[16,128]{1,0:T(8,128)(2,1)S(1)}) custom-call(f32[1,512]{1,0:T(1,128)S(1)} %bitcast.9, bf16[5120,512]{1,0:T(8,128)(2,1)S(1)} %bitcast.7, bf16[5120,512]{1,0:T(8,128)(2,1)S(1)} %get-tuple-element.33.other_ref, bf16[16,12,128]{2,1,0:T(8,128)(2,1)S(1)} %all_to_all.63.refs_0_.refs_1_.whole0_ref), custom_call_target="tpu_custom_call" | custom-call | flops 503316480 | bytes 10485760 | tf_op jit(solution)/shard_map/pallas_call | solution.py:167
  104.3 14.8 %all_to_all.64.refs_0_ = bf16[16,48,640]{2,1,0:T(8,128)(2,1)S(1)} all-to-all(bf16[16,48,640]{2,1,0:T(8,128)(2,1)S(1)} %get-tuple-element.40), channel_id=1, replica_groups=mesh['rows'=32,'feat'=16] {'feat'}, dimensions={0} | all-to-all | bytes 1966080 | tf_op jit(solution)/shard_map/all_to_all | solution.py:435
  119.3 14.6 %all_to_all.65.message_ref = bf16[16,256,128]{2,1,0:T(8,128)(2,1)S(1)} all-to-all(bf16[16,256,128]{2,1,0:T(8,128)(2,1)S(1)} %shard_map.74), channel_id=1, replica_groups=mesh['rows'=32,'feat'=16] {'feat'}, dimensions={0} | all-to-all | bytes 2097152 | tf_op jit(solution)/shard_map/all_to_all | solution.py:435
  133.9 1.9 shard_map.75
  135.8 15.3 %all_to_all.66.terms_ref = bf16[16,16,128]{2,1,0:T(8,128)(2,1)S(1)} all-to-all(bf16[16,16,128]{2,1,0:T(8,128)(2,1)S(1)} %get-tuple-element.42), channel_id=1, replica_groups={{0,32,64,96,128,160,192,224,256,288,320,352,384,416,448,480},{16,48,80,..., dimensions={0} | all-to-all | bytes 131072 | tf_op jit(solution)/shard_map/all_to_all | solution.py:438
  151.2 14.2 %all_to_all.67.refs_0_.whole1_ref = bf16[16,12,128]{2,1,0:T(8,128)(2,1)S(1)} all-to-all(bf16[16,12,128]{2,1,0:T(8,128)(2,1)S(1)} %get-tuple-element.46), channel_id=1, replica_groups={{0,32,64,96,128,160,192,224,256,288,320,352,384,416,448,480},{16,48,80,..., dimensions={0} | all-to-all | bytes 98304 | tf_op jit(solution)/shard_map/all_to_all | solution.py:438
  165.5 3.2 %shard_map.77 = (bf16[16,48,640]{2,1,0:T(8,128)(2,1)S(1)}, bf16[16,128]{1,0:T(8,128)(2,1)S(1)}) custom-call(f32[1,512]{1,0:T(1,128)S(1)} %bitcast.10, bf16[5120,512]{1,0:T(8,128)(2,1)S(1)} %bitcast.7, bf16[5120,512]{1,0:T(8,128)(2,1)S(1)} %get-tuple-element.33.other_ref, bf16[16,12,128]{2,1,0:T(8,128)(2,1)S(1)} %all_to_all.67.refs_0_.whole1_ref, ...), custom_call_target="tpu_custom_call" | custom-call | flops 503316480 | bytes 10485760 | tf_op jit(solution)/shard_map/pallas_call | solution.py:167
  168.6 14.1 %all_to_all.68.refs_0_ = bf16[16,48,640]{2,1,0:T(8,128)(2,1)S(1)} all-to-all(bf16[16,48,640]{2,1,0:T(8,128)(2,1)S(1)} %get-tuple-element.47), channel_id=1, replica_groups=mesh['rows'=32,'feat'=16] {'feat'}, dimensions={0} | all-to-all | bytes 1966080 | tf_op jit(solution)/shard_map/all_to_all | solution.py:435
  182.9 15.1 %all_to_all.69.message_ref = bf16[16,256,128]{2,1,0:T(8,128)(2,1)S(1)} all-to-all(bf16[16,256,128]{2,1,0:T(8,128)(2,1)S(1)} %shard_map.78), channel_id=1, replica_groups=mesh['rows'=32,'feat'=16] {'feat'}, dimensions={0} | all-to-all | bytes 2097152 | tf_op jit(solution)/shard_map/all_to_all | solution.py:435
  198.0 1.9 shard_map.79
  199.9 14.2 %all_to_all.70.terms_ref = bf16[16,16,128]{2,1,0:T(8,128)(2,1)S(1)} all-to-all(bf16[16,16,128]{2,1,0:T(8,128)(2,1)S(1)} %get-tuple-element.49), channel_id=1, replica_groups={{0,32,64,96,128,160,192,224,256,288,320,352,384,416,448,480},{16,48,80,..., dimensions={0} | all-to-all | bytes 131072 | tf_op jit(solution)/shard_map/all_to_all | solution.py:438
  214.3 14.2 %all_to_all.71.pieces_ref = bf16[16,16,128]{2,1,0:T(8,128)(2,1)S(1)} all-to-all(bf16[16,16,128]{2,1,0:T(8,128)(2,1)S(1)} %shard_map.80), channel_id=1, replica_groups={{0,32,64,96,128,160,192,224,256,288,320,352,384,416,448,480},{16,48,80,..., dimensions={0} | all-to-all | bytes 131072 | tf_op jit(solution)/shard_map/all_to_all | solution.py:438
  228.7 16.6 %collective-permute-start.2 = (f32[2,48,512]{2,1,0:T(8,128)S(1)}, f32[2,48,512]{2,1,0:T(8,128)S(1)}, u32[]{:S(2)}, u32[]{:S(2)}) collective-permute-start(f32[2,48,512]{2,1,0:T(8,128)S(1)} %shard_map.81.own_ref), channel_id=1, source_target_pairs={{0,16},{16,0},{32,48},{48,32},{64,80},{80,64},{96,112},{112,96},{1... | collective-permute-start | bytes 589832 | tf_op jit(solution)/shard_map/ppermute | solution.py:476
  245.3 1.0 collective-permute-done.2.other_ref
  (27 shorter events, 5.3 us)
Async XLA Ops:
  0.6 18.4 %collective-permute-start = (bf16[5120,512]{1,0:T(8,128)(2,1)}, bf16[5120,512]{1,0:T(8,128)(2,1)}, u32[]{:S(2)}, u32[]{:S(2)}) collective-permute-start(bf16[5120,512]{1,0:T(8,128)(2,1)} %own_ref.11), channel_id=1, source_target_pairs={{0,16},{16,0},{32,48},{48,32},{64,80},{80,64},{96,112},{112,96},{1... | collective-permute-start | bytes 15728648 | tf_op jit(solution)/shard_map/ppermute | solution.py:417
  11.2 11.5 %collective-permute-start.1 = (f32[96,640]{1,0:T(8,128)S(1)}, f32[96,640]{1,0:T(8,128)S(1)}, u32[]{:S(2)}, u32[]{:S(2)}) collective-permute-start(f32[96,640]{1,0:T(8,128)S(1)} %dynamic-slice_add_fusion.refs_1_), channel_id=1, source_target_pairs={{0,16},{16,0},{32,48},{48,32},{64,80},{80,64},{96,112},{112,96},{1... | collective-permute-start | bytes 737288 | tf_op jit(solution)/shard_map/ppermute | solution.py:429
  13.2 2.5 %copy-start = (bf16[5120,512]{1,0:T(8,128)(2,1)S(1)}, bf16[5120,512]{1,0:T(8,128)(2,1)}, u32[]{:S(2)}) copy-start(bf16[5120,512]{1,0:T(8,128)(2,1)} %own_ref.11) | copy-start | bytes 15728644
  15.7 0.9 copy-start.1
  16.6 0.7 copy-start.3
  17.3 42.5 %slice-start = ((s8[5242880]{0:T(1024)(128)(4,1)}), s8[4194304]{0:T(1024)(128)(4,1)S(1)}, s32[]{:S(2)}) async-start(s8[5242880]{0:T(1024)(128)(4,1)} %bitcast.6), calls=%async_computation.12 | async-start | bytes 8388608
  19.0 40.8 %slice-start.1 = ((s8[5242880]{0:T(1024)(128)(4,1)}), s8[1048576]{0:T(1024)(128)(4,1)S(1)}, s32[]{:S(2)}) async-start(s8[5242880]{0:T(1024)(128)(4,1)} %bitcast.6), calls=%async_computation.13 | async-start | bytes 2097152
  59.7 41.4 %copy-start.4 = (f32[512]{0:T(512)S(1)}, f32[512]{0:T(512)}, u32[]{:S(2)}) copy-start(f32[512]{0:T(512)} %param.9) | copy-start | bytes 6148
  198.0 30.5 %copy-start.2 = (f32[96,512]{1,0:T(8,128)S(1)}, f32[96,512]{1,0:T(8,128)}, u32[]{:S(2)}) copy-start(f32[96,512]{1,0:T(8,128)} %noise_ref.3) | copy-start | bytes 589828
  228.7 17.7 %collective-permute-start.2 = (f32[2,48,512]{2,1,0:T(8,128)S(1)}, f32[2,48,512]{2,1,0:T(8,128)S(1)}, u32[]{:S(2)}, u32[]{:S(2)}) collective-permute-start(f32[2,48,512]{2,1,0:T(8,128)S(1)} %shard_map.81.own_ref), channel_id=1, source_target_pairs={{0,16},{16,0},{32,48},{48,32},{64,80},{80,64},{96,112},{112,96},{1... | collective-permute-start | bytes 589832 | tf_op jit(solution)/shard_map/ppermute | solution.py:476
